TPU v7x, 32 devices: a whole 2x2x4 slice. The times are simulated.
32 devices in a mesh: rhs: 16 (over z, x, core), fac: 2 (over y).
Axes of the slice: x: 2, y: 2, z: 4, core: 2. Of those that a mesh axis runs over, the one named last changes fastest.
Arguments:
- right_sides: bfloat16 [1024, 768], P('rhs', 'fac'), may hold values from -6 to 6
- stripe: bfloat16 [768, 768], P('fac', 'rhs'), may hold values from -0.109375 to 0.109375
- inverses: float32 [2, 384, 384], P('fac'), may hold values from -2 to 2, as said below
- structure: int32 [2, 2], replicated, may hold values 0 or 1
- heater_wattages: bfloat16 [256, 1024], P(None, 'rhs'), may hold values from -0.25 to 0.25
Outputs:
- unknown_vector_results: bfloat16 [1024, 768], P('rhs', 'fac')
- thermal_field_reply: float32 [256, 768], P('rhs', 'fac')
Inputs may be any that keep to these rules, and one draw needn't show every extreme that they name: Each inverses[s] is lower triangular with its diagonal between 0.5 and 2.
All inputs are finite; a program needn't handle non-finite values.
Results may differ from a plain program's by a relative error of at most 0.0095.
Values may be sent and summed in bfloat16 or wider, within the bound.
A program may use at most 64 MiB of HBM per device.

v0:
```python
import jax
import jax.numpy as jnp
from jax import lax
from jax.sharding import PartitionSpec as P


def against_rows(left, right):
    return lax.dot_general(
        left, right, (((1,), (1,)), ((), ())), preferred_element_type=jnp.float32
    )


def body(right_sides, stripe, inverses, structure, heater_wattages):
    block_width = inverses.shape[1]
    supers_count = lax.axis_size("fac")
    resident_position = lax.axis_index("fac")
    right_hand_count = right_sides.shape[0]
    total_rows = block_width * supers_count
    stripe_rows, all_sides = (
        lax.all_gather(stripe, "fac", axis=0, tiled=True),
        lax.all_gather(right_sides, "fac", axis=1, tiled=True),
    )
    every_block_inverse = lax.all_gather(inverses, "fac", axis=0, tiled=True)
    whole = lax.all_gather(stripe_rows, "rhs", axis=1, tiled=True)
    forward_sweep = jnp.zeros((right_hand_count, total_rows), jnp.bfloat16)
    for block in range(supers_count):
        low = block * block_width
        col_mask = jnp.repeat(structure[block], block_width).astype(jnp.bfloat16)
        update = against_rows(forward_sweep * col_mask, whole[low : low + block_width])
        remainder = all_sides[:, low : low + block_width].astype(jnp.float32) - update
        finished_unknowns = jnp.dot(
            remainder, every_block_inverse[block].T, precision=lax.Precision.HIGHEST
        )
        forward_sweep = forward_sweep.at[:, low : low + block_width].set(
            finished_unknowns.astype(jnp.bfloat16)
        )
    unknown_vector_results = jnp.zeros((right_hand_count, total_rows), jnp.bfloat16)
    for block in range(supers_count - 1, -1, -1):
        low = block * block_width
        row_mask = jnp.repeat(structure[:, block], block_width).astype(jnp.bfloat16)
        update = jnp.dot(
            unknown_vector_results * row_mask,
            whole[:, low : low + block_width],
            preferred_element_type=jnp.float32,
        )
        remainder = forward_sweep[:, low : low + block_width].astype(jnp.float32) - update
        finished_unknowns = jnp.dot(
            remainder, every_block_inverse[block], precision=lax.Precision.HIGHEST
        )
        unknown_vector_results = unknown_vector_results.at[:, low : low + block_width].set(
            finished_unknowns.astype(jnp.bfloat16)
        )
    resident_panel = lax.dynamic_slice_in_dim(
        unknown_vector_results, resident_position * block_width, block_width, 1
    )
    thermal_field_reply = lax.psum_scatter(
        jnp.dot(heater_wattages, resident_panel, preferred_element_type=jnp.float32),
        "rhs",
        scatter_dimension=0,
        tiled=True,
    )
    return (resident_panel, thermal_field_reply)


def solution(mesh):
    placed = (P("rhs", "fac"), P("fac", "rhs"), P("fac", None, None), P(), P(None, "rhs"))
    return jax.shard_map(
        body,
        mesh=mesh,
        in_specs=placed,
        out_specs=(P("rhs", "fac"), P("rhs", "fac")),
        check_vma=False,
    )
```

profile of v0, /device:TPU:0, one launch (start us, length us, event | category | flops | bytes accessed | tf_op | source)
XLA Modules:
  0.0 146.0 jit_solution(7706581156529776256)
XLA Ops:
  7.2 0.0 copy-start
  7.2 0.0 all-gather.3.cloned.1.call-start
  7.2 7.3 %all_gather.13 = bf16[768,48]{0,1:T(8,128)(2,1)} all-gather(bf16[384,48]{0,1:T(8,128)(2,1)} %param.14), channel_id=1, replica_groups=mesh['rhs'=16,'fac'=2] {'fac'}, dimensions={0}, use_global_device_ids=true | all-gather | bytes 110592 | tf_op jit(solution)/shard_map/all_gather | solution.py:20
  14.5 0.0 all-gather.3.cloned.1.call-update
  14.5 0.0 all-gather.5.cloned.1.call-start
  14.6 0.7 all-gather.5.cloned.1.call-update
  15.3 0.0 reduce-scatter.4.cloned.1.call-start
  15.3 0.7 convert.6
  16.0 0.1 broadcast_in_dim.16
  16.1 0.1 broadcast_in_dim.17
  16.2 0.2 slice_reduce_fusion
  16.4 0.1 broadcast_in_dim.18
  16.5 0.1 broadcast_in_dim.19
  16.6 0.6 compare_reduce_fusion
  17.2 5.0 %all_gather.12 = bf16[64,768]{1,0:T(8,128)(2,1)S(1)} all-gather(bf16[64,384]{1,0:T(8,128)(2,1)} %param.13), channel_id=1, replica_groups=mesh['rhs'=16,'fac'=2] {'fac'}, dimensions={1}, use_global_device_ids=true | all-gather | bytes 147456 | tf_op jit(solution)/shard_map/all_gather | solution.py:21
  22.2 31.3 %all-gather.3.cloned.1.call-done = bf16[768,768]{0,1:T(8,128)(2,1)} async-done(((bf16[768,48]{0,1:T(8,128)(2,1)}), bf16[768,768]{0,1:T(8,128)(2,1)}) %all-gather.3.cloned.1.call-update) | async-done | bytes 1179664 | tf_op jit(solution)/shard_map/all_gather | solution.py:24
  53.4 0.0 copy-start.2
  53.4 1.4 convolution_subtract_fusion.3
  54.8 21.9 %all-gather.5.cloned.1.call-done = f32[2,384,384]{2,1,0:T(8,128)} async-done(((f32[1,384,384]{2,1,0:T(8,128)}), f32[2,384,384]{2,1,0:T(8,128)}) %all-gather.5.cloned.1.call-update) | async-done | bytes 1179664 | tf_op jit(solution)/shard_map/all_gather | solution.py:23
  76.7 0.0 copy-start.1
  76.7 2.5 %fusion.1 = bf16[64,384]{1,0:T(8,128)(2,1)S(1)} fusion(f32[64,384]{1,0:T(8,128)S(1)} %convolution_subtract_fusion.3, f32[2,384,384]{2,1,0:T(8,128)} %all-gather.5.cloned.1.call-done, pred[]{:T(512)} %compare_reduce_fusion), kind=kOutput, calls=%fused_computation.10 | convolution fusion | flops 113295360 | bytes 737792 | tf_op jit(solution)/shard_map/dot_general | solution.py:31
  79.3 0.0 copy-done.2
  79.3 0.2 convolution_subtract_fusion.2
  79.5 0.0 copy-done.1
  79.5 0.7 fusion
  80.3 0.3 convolution_subtract_fusion.1
  80.6 0.5 convolution_convert_fusion.1
  81.1 0.3 convolution_subtract_fusion
  81.4 1.1 fusion.2
  82.5 0.0 copy-done
  82.5 0.0 copy-start.3
  82.5 0.2 convolution_bitcast_fusion
  82.8 0.9 copy.9
  83.7 0.0 reduce-scatter.4.cloned.1.call-update
  83.7 55.7 %reduce-scatter.4.cloned.1.call-done = f32[16,384]{1,0:T(8,128)} async-done(((f32[256,384]{1,0:T(8,128)}), f32[16,384]{1,0:T(8,128)}) %reduce-scatter.4.cloned.1.call-update) | async-done | bytes 24592
  139.4 0.0 copy-done.3
  (6 shorter events, 0.1 us)
Async XLA Ops:
  7.2 75.4 %copy-start = (bf16[256,64]{0,1:T(8,128)(2,1)S(1)}, bf16[256,64]{0,1:T(8,128)(2,1)}, u32[]{:S(2)}) copy-start(bf16[256,64]{0,1:T(8,128)(2,1)} %param.17) | copy-start | bytes 98308
  7.2 46.2 %all-gather.3.cloned.1.call-start = ((), (), s32[]{:S(2)}) async-start(), calls=%async_computation.1 | async-start | bytes 1253376 | tf_op jit(solution)/shard_map/all_gather | solution.py:24
  14.5 62.2 %all-gather.5.cloned.1.call-start = ((), (), s32[]{:S(2)}) async-start(), calls=%async_computation.2 | async-start | bytes 1769472 | tf_op jit(solution)/shard_map/all_gather | solution.py:23
  15.3 124.2 %reduce-scatter.4.cloned.1.call-start = ((), (), s32[]{:S(2)}) async-start(), calls=%async_computation.3 | async-start | bytes 417792
  53.4 25.9 %copy-start.2 = (bf16[768,768]{0,1:T(8,128)(2,1)S(1)}, bf16[768,768]{0,1:T(8,128)(2,1)}, u32[]{:S(2)}) copy-start(bf16[768,768]{0,1:T(8,128)(2,1)} %all-gather.3.cloned.1.call-done) | copy-start | bytes 3538948
  76.7 2.8 %copy-start.1 = (f32[2,384,384]{2,1,0:T(8,128)S(1)}, f32[2,384,384]{2,1,0:T(8,128)}, u32[]{:S(2)}) copy-start(f32[2,384,384]{2,1,0:T(8,128)} %all-gather.5.cloned.1.call-done) | copy-start | bytes 3538948
  82.5 56.9 %copy-start.3 = (bf16[64,384]{1,0:T(8,128)(2,1)}, bf16[64,384]{1,0:T(8,128)(2,1)S(1)}, u32[]{:S(2)}) copy-start(bf16[64,384]{1,0:T(8,128)(2,1)S(1)} %fusion.11) | copy-start | bytes 147460
Sparse Core Ops, SparseCore 0:
  14.6 38.7 all-gather.2
  55.0 21.7 all-gather.4
  83.9 55.5 reduce-scatter.3
where the time goes:
time: 146 us
  waiting for transfers between devices  110 us (75%)
  between operations  13.8 us (9%)
  blocking collectives  12.2 us (8%)
  matrix products  7.3 us (5%)
  other arithmetic  1.55 us (1%)
    unnamed x4, waiting for transfers between devices  56.4 us
    all_gather x1, waiting for transfers between devices, body(): whole = lax.all_gather(stripe_rows, 'rhs', axis=1, tiled=True)  31.3 us
    all_gather x1, waiting for transfers between devices, body(): every_block_inverse = lax.all_gather(inverses, 'fac', axis=0, tiled=True)  21.9 us
    all_gather x1, blocking collectives, body(): lax.all_gather(stripe, 'fac', axis=0, tiled=True)  7.25 us
    all_gather x1, blocking collectives, body(): lax.all_gather(right_sides, 'fac', axis=1, tiled=True)  4.97 us
    dot_general x2, matrix products, body(): jnp.dot(remainder, every_block_inverse[block].T, precision=lax.Precision....  3.28 us
  transfers between devices with their start and end apart: 3, of which 3 were waited for; matrix products, arithmetic and copies ran while one was open for 2% of the time, Pallas kernels for 0%

commit v1 on v0

--- a/solution.py
+++ b/solution.py
@@ -1,7 +1,33 @@
+import functools
 import jax
 import jax.numpy as jnp
 from jax import lax
 from jax.sharding import PartitionSpec as P
+
+
+def cut_the_indices(shard_in, axis_no):
+    fresh = list(shard_in.shape[1:])
+    fresh[axis_no] *= shard_in.shape[0]
+    return jnp.moveaxis(shard_in, 0, axis_no).reshape(fresh)
+
+
+def spot_pair(own_rows, axis_id):
+    num = lax.axis_size(axis_id)
+    carry = own_rows[None]
+    for at in range(num.bit_length() - 1):
+        x_now = 1 << at
+        a_next = lax.ppermute(carry, axis_id, list(map(lambda ix: (ix, ix ^ x_now), range(num))))
+        all_values = jnp.stack([carry, a_next], 0)
+        lower = lax.axis_index(axis_id) >> at & 1
+        carry = jnp.where(lower == 0, all_values, all_values[::-1]).reshape(-1, *own_rows.shape)
+    return carry
+
+
+def push_edges_all(panel, sheet, dimension_no):
+    return cut_the_indices(spot_pair(panel, sheet), dimension_no)
+
+
+guide_case_by_axis = functools.partial(push_edges_all, sheet="fac", dimension_no=0)
 
 
 def against_rows(left, right):
@@ -20,7 +46,7 @@
         lax.all_gather(stripe, "fac", axis=0, tiled=True),
         lax.all_gather(right_sides, "fac", axis=1, tiled=True),
     )
-    every_block_inverse = lax.all_gather(inverses, "fac", axis=0, tiled=True)
+    every_block_inverse = guide_case_by_axis(inverses)
     whole = lax.all_gather(stripe_rows, "rhs", axis=1, tiled=True)
     forward_sweep = jnp.zeros((right_hand_count, total_rows), jnp.bfloat16)
     for block in range(supers_count):

time: 146 us -> 122 us (0.84)
  waiting for transfers between devices: 110 us -> 76.7 us
  blocking collectives: 12.2 us -> 20.2 us
    all_gather x1 -> x0, waiting for transfers between devices: 21.9 us -> none  [body(): every_block_inverse = lax.all_gather(inverses, 'fac', axis=0, tiled=True)]
    all_gather x1, waiting for transfers between devices: 31.3 us -> 22 us  [body(): whole = lax.all_gather(stripe_rows, 'rhs', axis=1, tiled=True)]
    all_gather x1, blocking collectives: 4.97 us -> 12.9 us  [body(): lax.all_gather(right_sides, 'fac', axis=1, tiled=True)]
    unnamed x4 -> x3, waiting for transfers between devices: 56.4 us -> 54.7 us
  transfers between devices with their start and end apart: 3 -> 3, of which waited for: 3 -> 2; matrix products, arithmetic and copies ran while one was open for 2% -> 3% of each run, Pallas kernels for 0% -> 0%
where the time goes in v1:
time: 122 us
  waiting for transfers between devices  76.7 us (63%)
  blocking collectives  20.2 us (17%)
  between operations  14.1 us (12%)
  matrix products  6.13 us (5%)
  other arithmetic  2.77 us (2%)
  local copies, waits for them, and re-layouts  1.3 us (1%)
    unnamed x3, waiting for transfers between devices  54.7 us
    all_gather x1, waiting for transfers between devices, body(): whole = lax.all_gather(stripe_rows, 'rhs', axis=1, tiled=True)  22 us
    all_gather x1, blocking collectives, body(): lax.all_gather(right_sides, 'fac', axis=1, tiled=True)  12.9 us
    all_gather x1, blocking collectives, body(): lax.all_gather(stripe, 'fac', axis=0, tiled=True)  7.25 us
  transfers between devices with their start and end apart: 3, of which 2 were waited for; matrix products, arithmetic and copies ran while one was open for 3% of the time, Pallas kernels for 0%

profile of v1, /device:TPU:0, one launch (start us, length us, event | category | flops | bytes accessed | tf_op | source)
XLA Modules:
  0.0 122.1 jit_solution(14752444318986038549)
XLA Ops:
  7.2 0.0 copy-start
  7.2 0.0 all-gather.2.cloned.1.call-start
  7.2 7.3 %all_gather.10 = bf16[768,48]{0,1:T(8,128)(2,1)} all-gather(bf16[384,48]{0,1:T(8,128)(2,1)} %param.14), channel_id=1, replica_groups=mesh['rhs'=16,'fac'=2] {'fac'}, dimensions={0}, use_global_device_ids=true | all-gather | bytes 110592 | tf_op jit(solution)/shard_map/all_gather | solution.py:46
  14.5 0.0 all-gather.2.cloned.1.call-update
  14.5 0.0 reduce-scatter.4.cloned.1.call-start
  14.6 0.7 collective-permute-start
  15.3 0.7 convert.6
  16.0 0.1 broadcast_in_dim.19
  16.1 0.1 broadcast_in_dim.21
  16.2 0.2 slice_reduce_fusion
  16.3 0.1 broadcast_in_dim.22
  16.4 0.1 broadcast_in_dim.23
  16.5 0.6 compare_reduce_fusion
  17.2 12.9 %all_gather.9 = bf16[64,768]{1,0:T(8,128)(2,1)S(1)} all-gather(bf16[64,384]{1,0:T(8,128)(2,1)} %param.13), channel_id=1, replica_groups=mesh['rhs'=16,'fac'=2] {'fac'}, dimensions={1}, use_global_device_ids=true | all-gather | bytes 147456 | tf_op jit(solution)/shard_map/all_gather | solution.py:47
  30.1 0.0 collective-permute-done
  30.1 1.1 pad_maximum_fusion
  31.2 0.1 reverse_select_fusion
  31.3 22.0 %all-gather.2.cloned.1.call-done = bf16[768,768]{0,1:T(8,128)(2,1)} async-done(((bf16[768,48]{0,1:T(8,128)(2,1)}), bf16[768,768]{0,1:T(8,128)(2,1)}) %all-gather.2.cloned.1.call-update) | async-done | bytes 1179664 | tf_op jit(solution)/shard_map/all_gather | solution.py:50
  53.4 0.0 copy-start.1
  53.4 1.4 %convolution_subtract_fusion.3 = f32[64,384]{1,0:T(8,128)S(1)} fusion(bf16[768,768]{0,1:T(8,128)(2,1)} %all-gather.2.cloned.1.call-done, bf16[64,768]{1,0:T(8,128)(2,1)S(1)} %all_gather.9, bf16[768]{0:T(1024)(128)(2,1)S(1)} %mul_broadcast_in_dim.24), kind=kOutput, calls=%fused_computation.6 | convolution fusion | flops 37797888 | bytes 738816 | tf_op jit(solution)/shard_map/dot_general | solution.py:34
  54.8 1.4 %fusion.1 = bf16[64,384]{1,0:T(8,128)(2,1)S(1)} fusion(f32[64,384]{1,0:T(8,128)S(1)} %convolution_subtract_fusion.3, f32[2,1,1,384,384]{4,3,2,1,0:T(8,128)S(1)} %reverse_select_fusion, pred[]{:T(512)} %compare_reduce_fusion), kind=kOutput, calls=%fused_computation.12 | convolution fusion | flops 113295360 | bytes 737281 | tf_op jit(solution)/shard_map/dot_general | solution.py:57
  56.1 0.0 copy-done.1
  56.2 0.2 convolution_subtract_fusion.2
  56.4 0.7 fusion
  57.1 0.3 convolution_subtract_fusion.1
  57.4 0.5 convolution_convert_fusion.1
  57.9 0.3 convolution_subtract_fusion
  58.2 1.1 fusion.2
  59.4 0.0 copy-done
  59.4 0.0 copy-start.2
  59.4 0.2 convolution_bitcast_fusion
  59.6 0.9 copy.9
  60.5 0.0 reduce-scatter.4.cloned.1.call-update
  60.6 54.7 %reduce-scatter.4.cloned.1.call-done = f32[16,384]{1,0:T(8,128)} async-done(((f32[256,384]{1,0:T(8,128)}), f32[16,384]{1,0:T(8,128)}) %reduce-scatter.4.cloned.1.call-update) | async-done | bytes 24592
  115.2 0.0 copy-done.2
  (6 shorter events, 0.1 us)
Async XLA Ops:
  7.2 52.2 %copy-start = (bf16[256,64]{0,1:T(8,128)(2,1)S(1)}, bf16[256,64]{0,1:T(8,128)(2,1)}, u32[]{:S(2)}) copy-start(bf16[256,64]{0,1:T(8,128)(2,1)} %param.17) | copy-start | bytes 98308
  7.2 46.2 %all-gather.2.cloned.1.call-start = ((), (), s32[]{:S(2)}) async-start(), calls=%async_computation.1 | async-start | bytes 1253376 | tf_op jit(solution)/shard_map/all_gather | solution.py:50
  14.5 100.7 %reduce-scatter.4.cloned.1.call-start = ((), (), s32[]{:S(2)}) async-start(), calls=%async_computation.2 | async-start | bytes 417792
  14.6 15.5 %collective-permute-start = (f32[1,1,384,384]{3,2,1,0:T(8,128)}, f32[1,1,384,384]{3,2,1,0:T(8,128)S(1)}, u32[]{:S(2)}, u32[]{:S(2)}) collective-permute-start(f32[1,1,384,384]{3,2,1,0:T(8,128)} %bitcast.24), channel_id=1, source_target_pairs={{0,1},{1,0},{2,3},{3,2},{4,5},{5,4},{6,7},{7,6},{8,9},{9,8},{10,11... | collective-permute-start | bytes 1769480 | tf_op jit(solution)/shard_map/ppermute | solution.py:19
  53.4 2.8 %copy-start.1 = (bf16[768,768]{0,1:T(8,128)(2,1)S(1)}, bf16[768,768]{0,1:T(8,128)(2,1)}, u32[]{:S(2)}) copy-start(bf16[768,768]{0,1:T(8,128)(2,1)} %all-gather.2.cloned.1.call-done) | copy-start | bytes 3538948
  59.4 55.8 %copy-start.2 = (bf16[64,384]{1,0:T(8,128)(2,1)}, bf16[64,384]{1,0:T(8,128)(2,1)S(1)}, u32[]{:S(2)}) copy-start(bf16[64,384]{1,0:T(8,128)(2,1)S(1)} %fusion.11) | copy-start | bytes 147460
Sparse Core Ops, SparseCore 0:
  14.6 38.6 all-gather.1
  60.7 54.4 reduce-scatter.3
